TPU v7x, 256 devices: a whole 4x4x8 slice. The times are simulated.
256 devices in a mesh: dp: 16 (over y, z_hi, core), seq: 16 (over x, z_lo).
Axes of the slice: x: 4, y: 4, z: 8 (z_hi: 2, z_lo: 4; z = z_hi * 4 + z_lo), core: 2. Of those that a mesh axis runs over, the one named last changes fastest.
Arguments:
- query: bfloat16 [16, 2048, 6144], P('dp', 'seq')
- latent: bfloat16 [16, 2048, 512], P('dp', 'seq'), may hold values from -6 to 6
- rope_key: bfloat16 [16, 2048, 64], P('dp', 'seq')
- grad_mantissa: bfloat16 [16, 2048, 4096], P('dp', 'seq'), may hold values from -6 to 6
- grad_exponent: int32 [16, 2048, 32], P('dp', 'seq'), may hold values from -3 to 3
- forward_out: bfloat16 [16, 2048, 4096], P('dp', 'seq'), may hold values from -6 to 6
- offsets: int32 [16], P('dp'), may hold values from 0 to 1023
- w_key: bfloat16 [512, 32, 128], P(None, 'seq'), may hold values from -0.25 to 0.25
- w_value: bfloat16 [512, 32, 128], P(None, 'seq'), may hold values from -0.25 to 0.25
Outputs:
- grad_query: bfloat16 [16, 2048, 6144], P('dp', 'seq')
- grad_latent: float32 [16, 2048, 512], P('dp', 'seq')
- grad_rope: float32 [16, 2048, 64], P('dp', 'seq')
- grad_w_key: float32 [512, 32, 128], P(None, 'seq')
- grad_w_value: float32 [512, 32, 128], P(None, 'seq')
Inputs may be any that keep to these rules, and one draw needn't show every extreme that they name: `grad_exponent`: the output gradient of one token and head is its 128 mantissa entries times 2 to this power. `offsets`: tokens before the offset are left padding; each of them attends only to itself.
All inputs are finite; a program needn't handle non-finite values.
Results may differ from a plain program's by a relative error of at most 0.02.
Values may be sent and summed in bfloat16 or wider, within the bound.
No kernel may reach another device: no remote copies, remote signals or barrier semaphores. Data moves between devices by JAX's collectives and lax.ppermute only.
A program may use at most 128 MiB of HBM per device.

v0:
```python
import functools

import jax
import jax.numpy as jnp
import numpy as np
from jax import lax
from jax.experimental import pallas as pl
from jax.experimental.pallas import tpu as pltpu
from jax.sharding import PartitionSpec as P

LATENT = 512
ROPE = 64
NOPE = 128
VDIM = 128
QK = NOPE + ROPE
TOK = 128
PAIR = 2 * QK
MSG = PAIR + 2 * VDIM
BLOCK = TOK + 16
SLAB = 4 * BLOCK
GROUPS = ((0, 1), (3, 2))
SCALE = QK ** (-0.5)
LOG2E = 1.4426950408889634
BIG = -1e30
NY, NZH, NC, NX, NZ = 4, 2, 2, 4, 4
BF, F32 = jnp.bfloat16, jnp.float32


def dot(a, b):
    return jnp.dot(a, b, preferred_element_type=F32)


def moves(dy=0, dc=0, dx=0, dz=0, ring=0):
    pairs = []
    shape = (NY, NZH, NC, NX, NZ)
    for index in np.ndindex(*shape):
        y, zh, c, x, z = index
        along = (zh * NZ + z + ring) % (NZH * NZ)
        dest = ((y + dy) % NY, along // NZ, (c + dc) % NC, (x + dx) % NX, (along + dz) % NZ)
        pairs.append((int(np.ravel_multi_index(index, shape)), int(np.ravel_multi_index(dest, shape))))
    return pairs


def send(value, **shift):
    return lax.ppermute(value, ("dp", "seq"), moves(**shift))


def trade(value, axis):
    groups = {
        "x": [[z + NZ * x for x in range(NX)] for z in range(NZ)],
        "z": [[z + NZ * x for z in range(NZ)] for x in range(NX)],
        "y": [[r + NZH * NC * y for y in range(NY)] for r in range(NZH * NC)],
    }[axis]
    return lax.all_to_all(value, "dp" if axis == "y" else "seq", 0, 0, axis_index_groups=groups)


def spread(value, axis):
    return trade(jnp.broadcast_to(value[None], (4, *value.shape)), axis)


def pack_kernel(groups, sc, q0, q1, m0, m1, f0, f1, ex, out):
    step = pl.program_id(0)
    for kk, (q, m, f) in enumerate(((q0, m0, f0), (q1, m1, f1))):
        rows = slice(kk * TOK, kk * TOK + TOK)
        exps = ex[...].T
        lane = lax.broadcasted_iota(jnp.int32, exps.shape, 1)
        grads, deltas = [], []
        for h in range(2):
            e = jnp.sum(jnp.where(lane == 2 * (step * NZ + ((sc[0] + groups[kk]) & 3)) + h, exps, 0), axis=1, keepdims=True)
            scale = jnp.left_shift(jnp.ones_like(e), e + 3).astype(F32) * 0.125
            part = slice(h * VDIM, (h + 1) * VDIM)
            g = (m[:, part].astype(F32) * scale).astype(BF)
            grads.append(g)
            prod = g.astype(F32) * f[:, part].astype(F32)
            d = jnp.sum(prod.T, axis=0, keepdims=True)
            hi = d.astype(BF).astype(F32)
            mid = (d - hi).astype(BF).astype(F32)
            row = lax.broadcasted_iota(jnp.int32, (16, TOK), 0)
            deltas.append(
                jnp.where(row == 0, hi, jnp.where(row == 1, mid, jnp.where(row == 2, d - hi - mid, 0.0)))
            )
        out[0, rows, :PAIR] = q[...]
        out[0, rows, PAIR : PAIR + VDIM] = grads[0]
        out[0, rows, PAIR + VDIM :] = grads[1]
        out[0, 2 * TOK :, kk * 256 : kk * 256 + 256] = jnp.concatenate(deltas, axis=1).astype(BF)
    out[0, 2 * TOK :, 512:] = jnp.zeros((16, MSG - 512), BF)


def pack(groups, sc, query, mantissa, exponent, saved):
    def at(kk):
        return lambda s, sc: (0, s * NZ + ((sc[0] + groups[kk]) & 3))

    return pl.pallas_call(
        functools.partial(pack_kernel, groups),
        grid_spec=pltpu.PrefetchScalarGridSpec(
            num_scalar_prefetch=1,
            grid=(4,),
            in_specs=[
                pl.BlockSpec((TOK, PAIR), at(0)),
                pl.BlockSpec((TOK, PAIR), at(1)),
                pl.BlockSpec((TOK, 256), at(0)),
                pl.BlockSpec((TOK, 256), at(1)),
                pl.BlockSpec((TOK, 256), at(0)),
                pl.BlockSpec((TOK, 256), at(1)),
                pl.BlockSpec((32, TOK), lambda s, sc: (0, 0)),
            ],
            out_specs=pl.BlockSpec((1, 2 * TOK + 16, MSG), lambda s, sc: (s, 0, 0)),
        ),
        out_shape=jax.ShapeDtypeStruct((4, 2 * TOK + 16, MSG), BF),
        cost_estimate=pl.CostEstimate(flops=2_000_000, bytes_accessed=4_000_000, transcendentals=0),
        name="pack",
    )(sc, query, query, mantissa, mantissa, saved, saved, exponent)


def attn_kernel(sc, *refs):
    msgs, lats, given = refs[0:2], refs[2:6], refs[6:10]
    dqs, gls, gkeep, gsend = refs[10:14], refs[14:18], refs[18], refs[19]
    lat, lat_t, kx, kx_t, acc, acc_r, w, w_t, kn, vs, qs, gs, dl, dkv, dq_scr, gw, s0, s1, s2, s3 = refs[20:]
    slabs = (s0, s1, s2, s3)
    kk = pl.program_id(0)
    z, off, core, x, y = sc[0], sc[1], sc[2], sc[3], sc[4]

    @pl.when(kk == 0)
    def _():
        for s in range(4):
            j = (x - s) & 3
            ropes = []
            for b in range(4):
                block = lats[s][b * BLOCK : b * BLOCK + TOK, :]
                lat[j, b * TOK : b * TOK + TOK, :] = block
                lat_t[j, :, b * TOK : b * TOK + TOK] = block.T
                packed = lats[s][b * BLOCK + TOK : b * BLOCK + BLOCK, :]
                ropes += [packed[:, ROPE * c : ROPE * c + ROPE] for c in range(8)]
            r = lax.broadcasted_iota(jnp.int32, (512, ROPE), 0)
            lane = lax.broadcasted_iota(jnp.int32, (512, ROPE), 1)
            blk = r >> 7
            pos = 512 * j + 128 * ((z - blk) & 3) + (r & 127)
            hide = ((lane == 0) & (pos < off)) | ((lane == 1 + j) & (blk > z))
            extra = jnp.where(hide, BIG, 0.0).astype(BF)
            both = jnp.concatenate([jnp.concatenate(ropes, axis=0), extra], axis=1)
            kx[j] = both
            kx_t[j] = both.T
            acc[j] = jnp.zeros((512, LATENT), F32)
            acc_r[j] = jnp.zeros((512, ROPE), F32)

    for k in range(4):

        @pl.when(kk == k)
        def _():
            w[...] = given[k][...]

    weights = w[...]
    w_t[...] = weights.T
    for j in range(4):
        kv = dot(lat[j], weights).astype(BF)
        for h in range(2):
            kn[h, j] = kv[:, h * 128 : h * 128 + 128]
            vs[h, j] = kv[:, 256 + h * 128 : 384 + h * 128]
    for n in range(2):

        @pl.when((kk >> 1) == n)
        def _():
            rows = pl.ds(pl.multiple_of((kk & 1) * TOK, TOK), TOK)
            for i in range(4):
                lane = lax.broadcasted_iota(jnp.int32, (TOK, ROPE), 1)
                ones = jnp.where((lane == 0) | (lane == 1 + i), 1.0, 0.0).astype(BF)
                for h in range(2):
                    qs[h, i] = jnp.concatenate([msgs[n][i, rows, h * QK : h * QK + QK], ones], axis=1)
                    gs[h, i] = msgs[n][i, rows, PAIR + h * VDIM : PAIR + (h + 1) * VDIM]
                    lanes = pl.ds(pl.multiple_of((2 * (kk & 1) + h) * TOK, TOK), TOK)
                    part = jnp.sum(msgs[n][i, 2 * TOK :, lanes].astype(F32), axis=0, keepdims=True)
                    dl[h, i] = jnp.broadcast_to(part, (8, TOK))

    r = lax.broadcasted_iota(jnp.int32, (128, 128), 0)
    c = lax.broadcasted_iota(jnp.int32, (128, 128), 1)
    for h in range(2):
        q = qs[h].reshape(512, 256)
        q_t = q.T
        peaks = [None] * 4
        for j in range(4):
            keys = jnp.concatenate([kn[h, j], kx[j]], axis=1)
            sj = dot(keys, q_t[:, 128 * j :])
            pos = 512 * j + 128 * z + r
            own = jnp.where(r <= c, sj[:128, :128], BIG)
            own = jnp.where((r == c) & (pos < off), 0.0, own)
            slabs[j][:128, :128] = own
            if j < 3:
                slabs[j][:128, 128:] = sj[:128, 128:]
            slabs[j][128:, :] = sj[128:, :]
            top = jnp.max(sj[128:, :], axis=0, keepdims=True)
            head = jnp.max(own, axis=0, keepdims=True)
            if j < 3:
                head = jnp.concatenate([head, jnp.max(sj[:128, 128:], axis=0, keepdims=True)], axis=1)
            top = jnp.maximum(top, head)
            for i in range(j, 4):
                piece = top[:, 128 * (i - j) : 128 * (i - j) + 128]
                peaks[i] = piece if peaks[i] is None else jnp.maximum(peaks[i], piece)
        peak = jnp.concatenate(peaks, axis=1)
        total = jnp.zeros((1, 512), F32)
        for j in range(4):
            e = jnp.exp2((slabs[j][...] - peak[:, 128 * j :]) * (SCALE * LOG2E))
            slabs[j][...] = e
            add = jnp.sum(e, axis=0, keepdims=True)
            if j:
                add = jnp.concatenate([jnp.zeros((1, 128 * j), F32), add], axis=1)
            total = total + add
        inv = 1.0 / total
        g_t = gs[h].reshape(512, VDIM).T
        gn_t = (g_t.astype(F32) * inv).astype(BF)
        gn = gn_t.T
        delta = jnp.concatenate([dl[h, i][:1] for i in range(4)], axis=1) * inv
        dq_t = jnp.zeros((QK, 512), F32)
        for j in range(4):
            cut = slice(128 * j, 512)
            e = slabs[j][...]
            dp = dot(vs[h, j], gn_t[:, cut])
            ds = (e * (dp - delta[:, cut])).astype(BF)
            dv = dot(e.astype(BF), gn[cut])
            dk = dot(ds, q[cut]) * SCALE
            dkv[j, :, h * 128 : h * 128 + 128] = dk[:, :NOPE].astype(BF)
            dkv[j, :, 256 + h * 128 : 384 + h * 128] = dv.astype(BF)
            acc_r[j] += dk[:, NOPE:QK]
            keys_t = jnp.concatenate([kn[h, j].T, kx_t[j][:ROPE]], axis=0)
            add = dot(keys_t, ds)
            if j:
                add = jnp.concatenate([jnp.zeros((QK, 128 * j), F32), add], axis=1)
            dq_t = dq_t + add
        dq = (dq_t * SCALE).T.astype(BF)
        for i in range(4):
            dq_scr[i, :, h * QK : h * QK + QK] = dq[128 * i : 128 * i + 128]

    total_w = None
    for j in range(4):
        both = dkv[j]
        acc[j] += dot(both, w_t[...])
        add = dot(lat_t[j], both)
        total_w = add if total_w is None else total_w + add
    gw[...] = total_w
    for i in range(4):
        dqs[i][...] = dq_scr[(x + i) & 3]
    for s in range(4):
        at = ((y + s) & 3) * 64
        gkeep[s, 0] = gw[pl.ds(pl.multiple_of(core * 256 + at, 64), 64), :].astype(BF)
        gsend[s, 0] = gw[pl.ds(pl.multiple_of((1 - core) * 256 + at, 64), 64), :].astype(BF)

    @pl.when(kk == 3)
    def _():
        for s in range(4):
            i = (x + s) & 3
            for b in range(4):
                gls[s][b * BLOCK : b * BLOCK + TOK, :] = acc[i, b * TOK : b * TOK + TOK, :].astype(BF)
                parts = [acc_r[i, b * TOK + 16 * c : b * TOK + 16 * c + 16, :] for c in range(8)]
                gls[s][b * BLOCK + TOK : b * BLOCK + BLOCK, :] = jnp.concatenate(parts, axis=1).astype(BF)


def attention(sc, msgs, lats, w_all):
    def whole(shape):
        return pl.BlockSpec(shape, lambda k, sc: (0,) * len(shape))

    slab = whole((SLAB, LATENT))
    in_specs = [whole((4, 2 * TOK + 16, MSG))] * 2 + [slab] * 4 + [whole((512, 512))] * 4
    args = [*msgs, *lats, *w_all]
    out_specs = [pl.BlockSpec((TOK, PAIR), lambda k, sc: (k, 0))] * 4
    out_shape = [jax.ShapeDtypeStruct((4 * TOK, PAIR), BF)] * 4
    out_specs += [slab] * 4 + [pl.BlockSpec((4, 1, 64, 512), lambda k, sc: (0, k, 0, 0))] * 2
    out_shape += [jax.ShapeDtypeStruct((SLAB, LATENT), BF)] * 4 + [jax.ShapeDtypeStruct((4, 4, 64, 512), BF)] * 2
    scratch = [
        pltpu.VMEM((4, 512, LATENT), BF),
        pltpu.VMEM((4, LATENT, 512), BF),
        pltpu.VMEM((4, 512, 128), BF),
        pltpu.VMEM((4, 128, 512), BF),
        pltpu.VMEM((4, 512, LATENT), F32),
        pltpu.VMEM((4, 512, ROPE), F32),
        pltpu.VMEM((512, 512), BF),
        pltpu.VMEM((512, 512), BF),
        pltpu.VMEM((2, 4, 512, 128), BF),
        pltpu.VMEM((2, 4, 512, 128), BF),
        pltpu.VMEM((2, 4, TOK, 256), BF),
        pltpu.VMEM((2, 4, TOK, VDIM), BF),
        pltpu.VMEM((2, 4, 8, TOK), F32),
        pltpu.VMEM((4, 512, 512), BF),
        pltpu.VMEM((4, TOK, PAIR), BF),
        pltpu.VMEM((512, 512), F32),
        pltpu.VMEM((512, 512), F32),
        pltpu.VMEM((512, 384), F32),
        pltpu.VMEM((512, 256), F32),
        pltpu.VMEM((512, 128), F32),
    ]
    outs = pl.pallas_call(
        attn_kernel,
        grid_spec=pltpu.PrefetchScalarGridSpec(
            num_scalar_prefetch=1, grid=(4,), in_specs=in_specs, out_specs=out_specs, scratch_shapes=scratch
        ),
        out_shape=out_shape,
        compiler_params=pltpu.CompilerParams(vmem_limit_bytes=56 * 1024 * 1024),
        cost_estimate=pl.CostEstimate(flops=50_000_000_000, bytes_accessed=14_000_000, transcendentals=5_400_000),
        name="attention",
    )(sc, *args)
    return outs[0:4], outs[4:8], outs[8], outs[9]


def unpack_kernel(sc, s0, s1, s2, s3, out):
    for kk, group in enumerate(GROUPS[0] + GROUPS[1]):
        for s, ref in enumerate((s0, s1, s2, s3)):
            lanes = pl.multiple_of((((sc[3] - s) & 3) * NZ + ((sc[0] + group) & 3)) * PAIR, 128)
            out[:, pl.ds(lanes, PAIR)] = ref[kk * TOK : kk * TOK + TOK, :]


def unpack(sc, pieces):
    spec = pl.BlockSpec(memory_space=pltpu.VMEM)
    return pl.pallas_call(
        unpack_kernel,
        in_specs=[pl.BlockSpec(memory_space=pltpu.SMEM)] + [spec] * 4,
        out_specs=spec,
        out_shape=jax.ShapeDtypeStruct((TOK, 16 * PAIR), BF),
        cost_estimate=pl.CostEstimate(flops=0, bytes_accessed=3_000_000, transcendentals=0),
        name="unpack",
    )(sc, *pieces)


def latents_kernel(b0, b1, b2, b3, out, out_rope):
    total = summed([b[...] for b in (b0, b1, b2, b3)])
    out[...] = total[:TOK]
    out_rope[...] = jnp.concatenate([total[TOK:, ROPE * c : ROPE * c + ROPE] for c in range(8)], axis=0).T


def finish_latents(pieces):
    spec = pl.BlockSpec(memory_space=pltpu.VMEM)
    return pl.pallas_call(
        latents_kernel,
        in_specs=[spec] * 4,
        out_specs=[spec] * 2,
        out_shape=[jax.ShapeDtypeStruct((TOK, LATENT), F32), jax.ShapeDtypeStruct((ROPE, TOK), F32)],
        cost_estimate=pl.CostEstimate(flops=20_000_000_000, bytes_accessed=1_000_000, transcendentals=0),
        name="finish_latents",
    )(*pieces)


def weights_kernel(sc, mine, other, out_k, out_v):
    core = sc[2]
    for base, ref in ((core, mine), (1 - core, other)):
        rows = pl.ds(pl.multiple_of(base * 256, 256), 256)
        for h in range(2):
            out_k[rows, h, :] = ref[:, h * 128 : h * 128 + 128].astype(F32)
            out_v[rows, h, :] = ref[:, 256 + h * 128 : 384 + h * 128].astype(F32)


def place_weights(sc, mine, other):
    spec = pl.BlockSpec(memory_space=pltpu.VMEM)
    return pl.pallas_call(
        weights_kernel,
        in_specs=[pl.BlockSpec(memory_space=pltpu.SMEM)] + [spec] * 2,
        out_specs=[spec] * 2,
        out_shape=[jax.ShapeDtypeStruct((512, 2, 128), F32)] * 2,
        cost_estimate=pl.CostEstimate(flops=0, bytes_accessed=2_000_000, transcendentals=0),
        name="place_weights",
    )(sc, mine, other)


def barrier(*values):
    return lax.optimization_barrier(values)


def summed(parts):
    total = parts[0].astype(F32)
    for n in range(1, len(parts)):
        total = total + parts[n].astype(F32)
    return total


def shards(query, latent, rope_key, grad_mantissa, grad_exponent, forward_out, offsets, w_key, w_value):
    dp, seq = lax.axis_index("dp"), lax.axis_index("seq")
    sc = jnp.stack([seq & 3, offsets[0], dp & 1, seq >> 2, dp >> 2]).astype(jnp.int32)

    ropes = rope_key[0].reshape(8, 16, ROPE).transpose(1, 0, 2).reshape(16, LATENT)
    own = jnp.concatenate([latent[0], ropes], axis=0)
    w_own = jnp.concatenate([w_key.reshape(LATENT, 256), w_value.reshape(LATENT, 256)], axis=1)
    near = [send(w_own, ring=-1), send(w_own, ring=1)]
    slab = jnp.concatenate([own] + [send(own, dz=s) for s in (1, 2, 3)], axis=0)

    inputs = (query[0], grad_mantissa[0], grad_exponent[0].T, forward_out[0])
    packed = pack(GROUPS[0], sc, *inputs)
    first = trade(packed, "x")
    slab, packed, *near = barrier(slab, packed, *near)
    lats = [slab] + [send(slab, dx=s) for s in (1, 2, 3)]

    first, w_held, packed = barrier(first, w_own, pack(GROUPS[1], sc, *inputs))
    far = jnp.concatenate([send(w_held[:256], ring=-2), send(w_held[256:], ring=2)], axis=0)
    second = trade(packed, "x")
    w_all = [w_own, near[0], far, near[1]]

    w_all = [w_all[k] for k in GROUPS[0] + GROUPS[1]]
    dqs, priors, keep, away = attention(sc, (first, second), lats, w_all)

    along_x = summed([priors[0]] + [send(priors[s], dx=s) for s in (1, 2, 3)]).astype(BF)
    blocks = along_x.reshape(NZ, BLOCK, LATENT)
    grad_latent, grad_rope = finish_latents([blocks[0]] + [send(blocks[s], dz=-s) for s in (1, 2, 3)])

    both = (keep.astype(F32) + send(away, dc=1).astype(F32)).astype(BF)
    partial = summed([both[0]] + [send(both[s], dy=s) for s in (1, 2, 3)]).astype(BF)
    by_group = {k: partial[n] for n, k in enumerate(GROUPS[0] + GROUPS[1])}
    own_heads = summed([by_group[0]] + [send(by_group[k], ring=(0, 1, 2, -1)[k]) for k in (1, 2, 3)]).astype(BF)
    grad_query = unpack(sc, [dqs[0]] + [send(dqs[s], dx=s) for s in (1, 2, 3)])
    own_heads = (own_heads.astype(F32) + send(own_heads, ring=4).astype(F32)).astype(BF)
    mine = spread(own_heads, "y").reshape(256, 512)
    total_key, total_value = place_weights(sc, mine, send(mine, dc=1))
    return grad_query[None], grad_latent[None], grad_rope.T[None], total_key, total_value


def solution(mesh):
    tokens = P("dp", "seq", None)
    heads = P(None, "seq", None)
    in_specs = (tokens,) * 6 + (P("dp"), heads, heads)
    out_specs = (tokens,) * 3 + (heads, heads)
    return jax.shard_map(shards, mesh=mesh, in_specs=in_specs, out_specs=out_specs, check_vma=False)
```

profile of v0, /device:TPU:40, one launch (start us, length us, event | category | flops | bytes accessed | tf_op | source)
XLA Modules:
  0.0 192.5 jit_solution(8040485402737628190)
XLA Ops:
  1.9 5.2 %pack.2 = bf16[4,272,640]{2,1,0:T(8,128)(2,1)} custom-call(s32[5]{0:T(128)} %stack.19.sc, bf16[128,6144]{1,0:T(8,128)(2,1)} %bitcast.49, bf16[128,6144]{1,0:T(8,128)(2,1)} %bitcast.50, bf16[128,4096]{1,0:T(8,128)(2,1)} %bitcast.53, bf16[128,4096]{1,0:T(8,128)(2,1)} %bitcast.54, bf16[128,4096]{1,0:T(8,128)(2,1)} %bitcast.57, bf16[128,4096]{1,0:T(8,128)(2,1)} %bitcast.58, ...), custom_call_target="tpu_custom_call" | custom-call | flops 2000000 | bytes 4000000 | tf_op jit(solution)/shard_map/pack/pallas_call | solution.py:93
  7.1 4.4 %all-to-all-start = ((bf16[4,272,640]{2,1,0:T(8,128)(2,1)}), bf16[4,272,640]{2,1,0:T(8,128)(2,1)S(1)}, u32[]{:S(2)}, u32[]{:S(2)}) async-start(bf16[4,272,640]{2,1,0:T(8,128)(2,1)} %pack.2), calls=%async_computation | async-start | bytes 2785280 | tf_op jit(solution)/shard_map/all_to_all | solution.py:54
  12.5 3.3 %collective-permute-start.1 = (bf16[144,512]{1,0:T(8,128)(2,1)}, bf16[144,512]{1,0:T(8,128)(2,1)}, u32[]{:S(2)}, u32[]{:S(2)}) collective-permute-start(bf16[144,512]{1,0:T(8,128)(2,1)} %pad_maximum_fusion.1), channel_id=1, source_target_pairs={{0,2},{1,3},{2,0},{3,1},{4,6},{5,7},{6,4},{7,5},{8,10},{9,11},{10,... | collective-permute-start | bytes 442376 | tf_op jit(solution)/shard_map/ppermute | solution.py:45
  15.8 2.8 %collective-permute-start = (bf16[144,512]{1,0:T(8,128)(2,1)}, bf16[144,512]{1,0:T(8,128)(2,1)}, u32[]{:S(2)}, u32[]{:S(2)}) collective-permute-start(bf16[144,512]{1,0:T(8,128)(2,1)} %pad_maximum_fusion.1), channel_id=1, source_target_pairs={{0,1},{1,2},{2,3},{3,0},{4,5},{5,6},{6,7},{7,4},{8,9},{9,10},{10,1... | collective-permute-start | bytes 442376 | tf_op jit(solution)/shard_map/ppermute | solution.py:45
  21.5 5.2 %pack.3 = bf16[4,272,640]{2,1,0:T(8,128)(2,1)} custom-call(s32[5]{0:T(128)} %stack.19.sc, bf16[128,6144]{1,0:T(8,128)(2,1)} %bitcast.51, bf16[128,6144]{1,0:T(8,128)(2,1)} %bitcast.52, bf16[128,4096]{1,0:T(8,128)(2,1)} %bitcast.55, bf16[128,4096]{1,0:T(8,128)(2,1)} %bitcast.56, bf16[128,4096]{1,0:T(8,128)(2,1)} %bitcast.59, bf16[128,4096]{1,0:T(8,128)(2,1)} %bitcast.60, ...), custom_call_target="tpu_custom_call" | custom-call | flops 2000000 | bytes 4000000 | tf_op jit(solution)/shard_map/pack/pallas_call | solution.py:93
  26.7 3.6 %all-to-all-done.refs_0_ = bf16[4,272,640]{2,1,0:T(8,128)(2,1)S(1)} async-done(((bf16[4,272,640]{2,1,0:T(8,128)(2,1)}), bf16[4,272,640]{2,1,0:T(8,128)(2,1)S(1)}, u32[]{:S(2)}, u32[]{:S(2)}) %all-to-all-start) | async-done | bytes 1392672 | tf_op jit(solution)/shard_map/all_to_all | solution.py:54
  30.3 3.5 %all-to-all-start.1 = ((bf16[4,272,640]{2,1,0:T(8,128)(2,1)}), bf16[4,272,640]{2,1,0:T(8,128)(2,1)S(1)}, u32[]{:S(2)}, u32[]{:S(2)}) async-start(bf16[4,272,640]{2,1,0:T(8,128)(2,1)} %pack.3), calls=%async_computation.1 | async-start | bytes 2785280 | tf_op jit(solution)/shard_map/all_to_all | solution.py:54
  39.5 3.0 %collective-permute-start.7 = (bf16[576,512]{1,0:T(8,128)(2,1)}, bf16[576,512]{1,0:T(8,128)(2,1)S(1)}, u32[]{:S(2)}, u32[]{:S(2)}) collective-permute-start(bf16[576,512]{1,0:T(8,128)(2,1)} %constant_dynamic-update-slice_fusion.refs_2_), channel_id=1, source_target_pairs={{0,12},{1,13},{2,14},{3,15},{4,0},{5,1},{6,2},{7,3},{8,4},{9,5},{1... | collective-permute-start | bytes 1769480 | tf_op jit(solution)/shard_map/ppermute | solution.py:45
  44.2 4.6 %collective-permute-start.8 = (bf16[256,512]{1,0:T(8,128)(2,1)S(1)}, bf16[256,512]{1,0:T(8,128)(2,1)S(1)}, u32[]{:S(2)}, u32[]{:S(2)}) collective-permute-start(bf16[256,512]{1,0:T(8,128)(2,1)S(1)} %get-tuple-element.52), channel_id=1, source_target_pairs={{0,34},{1,35},{2,0},{3,1},{4,38},{5,39},{6,4},{7,5},{8,42},{9,43},... | collective-permute-start | bytes 786440 | tf_op jit(solution)/shard_map/ppermute | solution.py:45
  48.7 9.2 %collective-permute-done.8 = bf16[256,512]{1,0:T(8,128)(2,1)S(1)} collective-permute-done((bf16[256,512]{1,0:T(8,128)(2,1)S(1)}, bf16[256,512]{1,0:T(8,128)(2,1)S(1)}, u32[]{:S(2)}, u32[]{:S(2)}) %collective-permute-start.8) | collective-permute-done | bytes 262176 | tf_op jit(solution)/shard_map/ppermute | solution.py:45
  58.8 6.4 %collective-permute-done.7.refs_5_ = bf16[576,512]{1,0:T(8,128)(2,1)S(1)} collective-permute-done((bf16[576,512]{1,0:T(8,128)(2,1)}, bf16[576,512]{1,0:T(8,128)(2,1)S(1)}, u32[]{:S(2)}, u32[]{:S(2)}) %collective-permute-start.7) | collective-permute-done | bytes 589856 | tf_op jit(solution)/shard_map/ppermute | solution.py:45
  67.6 9.2 %collective-permute-done.5.refs_3_ = bf16[576,512]{1,0:T(8,128)(2,1)} collective-permute-done((bf16[576,512]{1,0:T(8,128)(2,1)}, bf16[576,512]{1,0:T(8,128)(2,1)}, u32[]{:S(2)}, u32[]{:S(2)}) %collective-permute-start.5) | collective-permute-done | bytes 589856 | tf_op jit(solution)/shard_map/ppermute | solution.py:45
  77.9 42.3 %attention.1 = (bf16[512,384]{1,0:T(8,128)(2,1)}, bf16[512,384]{1,0:T(8,128)(2,1)}, bf16[512,384]{1,0:T(8,128)(2,1)}, bf16[512,384]{1,0:T(8,128)(2,1)}, bf16[576...) custom-call(s32[5]{0:T(128)} %stack.19.sc, ...), custom_call_target="tpu_custom_call" | custom-call | flops 49999998976 | bytes 14000000 | tf_op jit(solution)/shard_map/attention/pallas_call | solution.py:289
  120.3 2.9 %collective-permute-done.19 = bf16[4,4,64,512]{3,2,1,0:T(8,128)(2,1)S(1)} collective-permute-done((bf16[4,4,64,512]{3,2,1,0:T(8,128)(2,1)}, bf16[4,4,64,512]{3,2,1,0:T(8,128)(2,1)S(1)}, u32[]{:S(2)}, u32[]{:S(2)}) %collective-permute-start.19) | collective-permute-done | bytes 1048608 | tf_op jit(solution)/shard_map/ppermute | solution.py:45
  127.0 2.3 %collective-permute-start.21 = (bf16[4,64,512]{2,1,0:T(8,128)(2,1)S(1)}, bf16[4,64,512]{2,1,0:T(8,128)(2,1)S(1)}, u32[]{:S(2)}, u32[]{:S(2)}) collective-permute-start(bf16[4,64,512]{2,1,0:T(8,128)(2,1)S(1)} %get-tuple-element.47), channel_id=1, source_target_pairs={{0,128},{1,129},{2,130},{3,131},{4,132},{5,133},{6,134},{7,135},{8... | collective-permute-start | bytes 786440 | tf_op jit(solution)/shard_map/ppermute | solution.py:45
  134.2 2.2 %collective-permute-start.15 = (bf16[576,512]{1,0:T(8,128)(2,1)S(1)}, bf16[576,512]{1,0:T(8,128)(2,1)S(1)}, u32[]{:S(2)}, u32[]{:S(2)}) collective-permute-start(bf16[576,512]{1,0:T(8,128)(2,1)S(1)} %copy-done.13), channel_id=1, source_target_pairs={{0,12},{1,13},{2,14},{3,15},{4,0},{5,1},{6,2},{7,3},{8,4},{9,5},{1... | collective-permute-start | bytes 1769480 | tf_op jit(solution)/shard_map/ppermute | solution.py:45
  136.4 4.6 %collective-permute-done.21 = bf16[4,64,512]{2,1,0:T(8,128)(2,1)S(1)} collective-permute-done((bf16[4,64,512]{2,1,0:T(8,128)(2,1)S(1)}, bf16[4,64,512]{2,1,0:T(8,128)(2,1)S(1)}, u32[]{:S(2)}, u32[]{:S(2)}) %collective-permute-start.21) | collective-permute-done | bytes 262176 | tf_op jit(solution)/shard_map/ppermute | solution.py:45
  145.5 4.0 %collective-permute-start.24 = (bf16[64,512]{1,0:T(8,128)(2,1)S(1)}, bf16[64,512]{1,0:T(8,128)(2,1)S(1)}, u32[]{:S(2)}, u32[]{:S(2)}) collective-permute-start(bf16[64,512]{1,0:T(8,128)(2,1)S(1)} %get-tuple-element.56), channel_id=1, source_target_pairs={{0,2},{1,3},{2,32},{3,33},{4,6},{5,7},{6,36},{7,37},{8,10},{9,11},... | collective-permute-start | bytes 196616 | tf_op jit(solution)/shard_map/ppermute | solution.py:45
  151.2 2.6 %collective-permute-done.24 = bf16[64,512]{1,0:T(8,128)(2,1)S(1)} collective-permute-done((bf16[64,512]{1,0:T(8,128)(2,1)S(1)}, bf16[64,512]{1,0:T(8,128)(2,1)S(1)}, u32[]{:S(2)}, u32[]{:S(2)}) %collective-permute-start.24) | collective-permute-done | bytes 65568 | tf_op jit(solution)/shard_map/ppermute | solution.py:45
  154.4 3.5 %collective-permute-start.12 = (bf16[512,384]{1,0:T(8,128)(2,1)S(1)}, bf16[512,384]{1,0:T(8,128)(2,1)S(1)}, u32[]{:S(2)}, u32[]{:S(2)}) collective-permute-start(bf16[512,384]{1,0:T(8,128)(2,1)S(1)} %copy-done.18), channel_id=1, source_target_pairs={{0,12},{1,13},{2,14},{3,15},{4,0},{5,1},{6,2},{7,3},{8,4},{9,5},{1... | collective-permute-start | bytes 1179656 | tf_op jit(solution)/shard_map/ppermute | solution.py:45
  160.0 6.3 %collective-permute-start.26 = (bf16[64,512]{1,0:T(8,128)(2,1)S(1)}, bf16[64,512]{1,0:T(8,128)(2,1)S(1)}, u32[]{:S(2)}, u32[]{:S(2)}) collective-permute-start(bf16[64,512]{1,0:T(8,128)(2,1)S(1)} %fusion.5), channel_id=1, source_target_pairs={{0,32},{1,33},{2,34},{3,35},{4,36},{5,37},{6,38},{7,39},{8,40},{9,... | collective-permute-start | bytes 196616 | tf_op jit(solution)/shard_map/ppermute | solution.py:45
  169.3 4.7 %all-to-all-start.2 = ((bf16[4,64,512]{2,1,0:T(8,128)(2,1)}), bf16[4,64,512]{2,1,0:T(8,128)(2,1)S(1)}, u32[]{:S(2)}, u32[]{:S(2)}) async-start(bf16[4,64,512]{2,1,0:T(8,128)(2,1)} %broadcast_in_dim.18), calls=%async_computation.2 | async-start | bytes 524288 | tf_op jit(solution)/shard_map/all_to_all | solution.py:54
  180.5 2.6 %unpack.1 = bf16[128,6144]{1,0:T(8,128)(2,1)} custom-call(s32[5]{0:T(128)} %stack.19.sc, bf16[512,384]{1,0:T(8,128)(2,1)} %get-tuple-element.31.s0, bf16[512,384]{1,0:T(8,128)(2,1)} %copy-done.6, bf16[512,384]{1,0:T(8,128)(2,1)} %copy-done.7, bf16[512,384]{1,0:T(8,128)(2,1)} %copy-done.8), custom_call_target="tpu_custom_call" | custom-call | bytes 3000000 | tf_op jit(solution)/shard_map/unpack/pallas_call | solution.py:311
  190.0 2.5 %place_weights.1 = (f32[512,2,128]{2,1,0:T(2,128)}, f32[512,2,128]{2,1,0:T(2,128)}) custom-call(s32[5]{0:T(128)} %stack.19.sc, bf16[256,512]{1,0:T(8,128)(2,1)} %bitcast.63, bf16[256,512]{1,0:T(8,128)(2,1)} %copy-done.9), custom_call_target="tpu_custom_call" | custom-call | bytes 2000000 | tf_op jit(solution)/shard_map/place_weights/pallas_call | solution.py:350
  (113 shorter events, 49.9 us)
Async XLA Ops:
  7.1 23.2 %all-to-all-start = ((bf16[4,272,640]{2,1,0:T(8,128)(2,1)}), bf16[4,272,640]{2,1,0:T(8,128)(2,1)S(1)}, u32[]{:S(2)}, u32[]{:S(2)}) async-start(bf16[4,272,640]{2,1,0:T(8,128)(2,1)} %pack.2), calls=%async_computation | async-start | bytes 2785280 | tf_op jit(solution)/shard_map/all_to_all | solution.py:54
  12.4 25.2 %collective-permute-start.2 = (bf16[144,512]{1,0:T(8,128)(2,1)}, bf16[144,512]{1,0:T(8,128)(2,1)S(1)}, u32[]{:S(2)}, u32[]{:S(2)}) collective-permute-start(bf16[144,512]{1,0:T(8,128)(2,1)} %pad_maximum_fusion.1), channel_id=1, source_target_pairs={{0,3},{1,0},{2,1},{3,2},{4,7},{5,4},{6,5},{7,6},{8,11},{9,8},{10,9... | collective-permute-start | bytes 442376 | tf_op jit(solution)/shard_map/ppermute | solution.py:45
  12.5 23.5 %collective-permute-start.1 = (bf16[144,512]{1,0:T(8,128)(2,1)}, bf16[144,512]{1,0:T(8,128)(2,1)}, u32[]{:S(2)}, u32[]{:S(2)}) collective-permute-start(bf16[144,512]{1,0:T(8,128)(2,1)} %pad_maximum_fusion.1), channel_id=1, source_target_pairs={{0,2},{1,3},{2,0},{3,1},{4,6},{5,7},{6,4},{7,5},{8,10},{9,11},{10,... | collective-permute-start | bytes 442376 | tf_op jit(solution)/shard_map/ppermute | solution.py:45
  15.8 18.6 %collective-permute-start = (bf16[144,512]{1,0:T(8,128)(2,1)}, bf16[144,512]{1,0:T(8,128)(2,1)}, u32[]{:S(2)}, u32[]{:S(2)}) collective-permute-start(bf16[144,512]{1,0:T(8,128)(2,1)} %pad_maximum_fusion.1), channel_id=1, source_target_pairs={{0,1},{1,2},{2,3},{3,0},{4,5},{5,6},{6,7},{7,4},{8,9},{9,10},{10,1... | collective-permute-start | bytes 442376 | tf_op jit(solution)/shard_map/ppermute | solution.py:45
  18.7 20.7 %collective-permute-start.4 = (bf16[512,512]{1,0:T(8,128)(2,1)S(1)}, bf16[512,512]{1,0:T(8,128)(2,1)}, u32[]{:S(2)}, u32[]{:S(2)}) collective-permute-start(bf16[512,512]{1,0:T(8,128)(2,1)S(1)} %bitcast_dynamic-update-slice_fusion.refs_6_), channel_id=1, source_target_pairs={{0,1},{1,2},{2,3},{3,32},{4,5},{5,6},{6,7},{7,36},{8,9},{9,10},{10... | collective-permute-start | bytes 1572872 | tf_op jit(solution)/shard_map/ppermute | solution.py:45
  18.8 20.6 %collective-permute-start.3 = (bf16[512,512]{1,0:T(8,128)(2,1)S(1)}, bf16[512,512]{1,0:T(8,128)(2,1)}, u32[]{:S(2)}, u32[]{:S(2)}) collective-permute-start(bf16[512,512]{1,0:T(8,128)(2,1)S(1)} %bitcast_dynamic-update-slice_fusion.refs_6_), channel_id=1, source_target_pairs={{0,35},{1,0},{2,1},{3,2},{4,39},{5,4},{6,5},{7,6},{8,43},{9,8},{10... | collective-permute-start | bytes 1572872 | tf_op jit(solution)/shard_map/ppermute | solution.py:45
  30.3 46.5 %all-to-all-start.1 = ((bf16[4,272,640]{2,1,0:T(8,128)(2,1)}), bf16[4,272,640]{2,1,0:T(8,128)(2,1)S(1)}, u32[]{:S(2)}, u32[]{:S(2)}) async-start(bf16[4,272,640]{2,1,0:T(8,128)(2,1)} %pack.3), calls=%async_computation.1 | async-start | bytes 2785280 | tf_op jit(solution)/shard_map/all_to_all | solution.py:54
  39.5 25.8 %collective-permute-start.7 = (bf16[576,512]{1,0:T(8,128)(2,1)}, bf16[576,512]{1,0:T(8,128)(2,1)S(1)}, u32[]{:S(2)}, u32[]{:S(2)}) collective-permute-start(bf16[576,512]{1,0:T(8,128)(2,1)} %constant_dynamic-update-slice_fusion.refs_2_), channel_id=1, source_target_pairs={{0,12},{1,13},{2,14},{3,15},{4,0},{5,1},{6,2},{7,3},{8,4},{9,5},{1... | collective-permute-start | bytes 1769480 | tf_op jit(solution)/shard_map/ppermute | solution.py:45
  42.4 24.3 %collective-permute-start.6 = (bf16[576,512]{1,0:T(8,128)(2,1)}, bf16[576,512]{1,0:T(8,128)(2,1)S(1)}, u32[]{:S(2)}, u32[]{:S(2)}) collective-permute-start(bf16[576,512]{1,0:T(8,128)(2,1)} %constant_dynamic-update-slice_fusion.refs_2_), channel_id=1, source_target_pairs={{0,8},{1,9},{2,10},{3,11},{4,12},{5,13},{6,14},{7,15},{8,0},{9,1},... | collective-permute-start | bytes 1769480 | tf_op jit(solution)/shard_map/ppermute | solution.py:45
  43.3 33.5 %collective-permute-start.5 = (bf16[576,512]{1,0:T(8,128)(2,1)}, bf16[576,512]{1,0:T(8,128)(2,1)}, u32[]{:S(2)}, u32[]{:S(2)}) collective-permute-start(bf16[576,512]{1,0:T(8,128)(2,1)} %constant_dynamic-update-slice_fusion.refs_2_), channel_id=1, source_target_pairs={{0,4},{1,5},{2,6},{3,7},{4,8},{5,9},{6,10},{7,11},{8,12},{9,13},{1... | collective-permute-start | bytes 1769480 | tf_op jit(solution)/shard_map/ppermute | solution.py:45
  44.2 13.7 %collective-permute-start.8 = (bf16[256,512]{1,0:T(8,128)(2,1)S(1)}, bf16[256,512]{1,0:T(8,128)(2,1)S(1)}, u32[]{:S(2)}, u32[]{:S(2)}) collective-permute-start(bf16[256,512]{1,0:T(8,128)(2,1)S(1)} %get-tuple-element.52), channel_id=1, source_target_pairs={{0,34},{1,35},{2,0},{3,1},{4,38},{5,39},{6,4},{7,5},{8,42},{9,43},... | collective-permute-start | bytes 786440 | tf_op jit(solution)/shard_map/ppermute | solution.py:45
  48.7 9.3 %collective-permute-start.9 = (bf16[256,512]{1,0:T(8,128)(2,1)S(1)}, bf16[256,512]{1,0:T(8,128)(2,1)S(1)}, u32[]{:S(2)}, u32[]{:S(2)}) collective-permute-start(bf16[256,512]{1,0:T(8,128)(2,1)S(1)} %get-tuple-element.53), channel_id=1, source_target_pairs={{0,2},{1,3},{2,32},{3,33},{4,6},{5,7},{6,36},{7,37},{8,10},{9,11},... | collective-permute-start | bytes 786440 | tf_op jit(solution)/shard_map/ppermute | solution.py:45
  124.9 9.2 %collective-permute-start.20 = (bf16[4,64,512]{2,1,0:T(8,128)(2,1)S(1)}, bf16[4,64,512]{2,1,0:T(8,128)(2,1)S(1)}, u32[]{:S(2)}, u32[]{:S(2)}) collective-permute-start(bf16[4,64,512]{2,1,0:T(8,128)(2,1)S(1)} %get-tuple-element.45), channel_id=1, source_target_pairs={{0,64},{1,65},{2,66},{3,67},{4,68},{5,69},{6,70},{7,71},{8,72},{9,... | collective-permute-start | bytes 786440 | tf_op jit(solution)/shard_map/ppermute | solution.py:45
  126.6 9.8 %collective-permute-start.22 = (bf16[4,64,512]{2,1,0:T(8,128)(2,1)S(1)}, bf16[4,64,512]{2,1,0:T(8,128)(2,1)S(1)}, u32[]{:S(2)}, u32[]{:S(2)}) collective-permute-start(bf16[4,64,512]{2,1,0:T(8,128)(2,1)S(1)} %get-tuple-element.46), channel_id=1, source_target_pairs={{0,192},{1,193},{2,194},{3,195},{4,196},{5,197},{6,198},{7,199},{8... | collective-permute-start | bytes 786440 | tf_op jit(solution)/shard_map/ppermute | solution.py:45
  127.0 14.0 %collective-permute-start.21 = (bf16[4,64,512]{2,1,0:T(8,128)(2,1)S(1)}, bf16[4,64,512]{2,1,0:T(8,128)(2,1)S(1)}, u32[]{:S(2)}, u32[]{:S(2)}) collective-permute-start(bf16[4,64,512]{2,1,0:T(8,128)(2,1)S(1)} %get-tuple-element.47), channel_id=1, source_target_pairs={{0,128},{1,129},{2,130},{3,131},{4,132},{5,133},{6,134},{7,135},{8... | collective-permute-start | bytes 786440 | tf_op jit(solution)/shard_map/ppermute | solution.py:45
  129.3 25.0 %collective-permute-start.13 = (bf16[576,512]{1,0:T(8,128)(2,1)S(1)}, bf16[576,512]{1,0:T(8,128)(2,1)S(1)}, u32[]{:S(2)}, u32[]{:S(2)}) collective-permute-start(bf16[576,512]{1,0:T(8,128)(2,1)S(1)} %copy-done.15), channel_id=1, source_target_pairs={{0,4},{1,5},{2,6},{3,7},{4,8},{5,9},{6,10},{7,11},{8,12},{9,13},{1... | collective-permute-start | bytes 1769480 | tf_op jit(solution)/shard_map/ppermute | solution.py:45
  131.0 29.0 %collective-permute-start.14 = (bf16[576,512]{1,0:T(8,128)(2,1)S(1)}, bf16[576,512]{1,0:T(8,128)(2,1)S(1)}, u32[]{:S(2)}, u32[]{:S(2)}) collective-permute-start(bf16[576,512]{1,0:T(8,128)(2,1)S(1)} %copy-done.14), channel_id=1, source_target_pairs={{0,8},{1,9},{2,10},{3,11},{4,12},{5,13},{6,14},{7,15},{8,0},{9,1},... | collective-permute-start | bytes 1769480 | tf_op jit(solution)/shard_map/ppermute | solution.py:45
  134.2 32.1 %collective-permute-start.15 = (bf16[576,512]{1,0:T(8,128)(2,1)S(1)}, bf16[576,512]{1,0:T(8,128)(2,1)S(1)}, u32[]{:S(2)}, u32[]{:S(2)}) collective-permute-start(bf16[576,512]{1,0:T(8,128)(2,1)S(1)} %copy-done.13), channel_id=1, source_target_pairs={{0,12},{1,13},{2,14},{3,15},{4,0},{5,1},{6,2},{7,3},{8,4},{9,5},{1... | collective-permute-start | bytes 1769480 | tf_op jit(solution)/shard_map/ppermute | solution.py:45
  149.5 29.2 %collective-permute-start.10 = (bf16[512,384]{1,0:T(8,128)(2,1)}, bf16[512,384]{1,0:T(8,128)(2,1)S(1)}, u32[]{:S(2)}, u32[]{:S(2)}) collective-permute-start(bf16[512,384]{1,0:T(8,128)(2,1)} %get-tuple-element.32), channel_id=1, source_target_pairs={{0,4},{1,5},{2,6},{3,7},{4,8},{5,9},{6,10},{7,11},{8,12},{9,13},{1... | collective-permute-start | bytes 1179656 | tf_op jit(solution)/shard_map/ppermute | solution.py:45
  153.8 25.8 %collective-permute-start.11 = (bf16[512,384]{1,0:T(8,128)(2,1)S(1)}, bf16[512,384]{1,0:T(8,128)(2,1)S(1)}, u32[]{:S(2)}, u32[]{:S(2)}) collective-permute-start(bf16[512,384]{1,0:T(8,128)(2,1)S(1)} %copy-done.19), channel_id=1, source_target_pairs={{0,8},{1,9},{2,10},{3,11},{4,12},{5,13},{6,14},{7,15},{8,0},{9,1},... | collective-permute-start | bytes 1179656 | tf_op jit(solution)/shard_map/ppermute | solution.py:45
  154.4 25.2 %collective-permute-start.12 = (bf16[512,384]{1,0:T(8,128)(2,1)S(1)}, bf16[512,384]{1,0:T(8,128)(2,1)S(1)}, u32[]{:S(2)}, u32[]{:S(2)}) collective-permute-start(bf16[512,384]{1,0:T(8,128)(2,1)S(1)} %copy-done.18), channel_id=1, source_target_pairs={{0,12},{1,13},{2,14},{3,15},{4,0},{5,1},{6,2},{7,3},{8,4},{9,5},{1... | collective-permute-start | bytes 1179656 | tf_op jit(solution)/shard_map/ppermute | solution.py:45
  160.0 8.5 %collective-permute-start.26 = (bf16[64,512]{1,0:T(8,128)(2,1)S(1)}, bf16[64,512]{1,0:T(8,128)(2,1)S(1)}, u32[]{:S(2)}, u32[]{:S(2)}) collective-permute-start(bf16[64,512]{1,0:T(8,128)(2,1)S(1)} %fusion.5), channel_id=1, source_target_pairs={{0,32},{1,33},{2,34},{3,35},{4,36},{5,37},{6,38},{7,39},{8,40},{9,... | collective-permute-start | bytes 196616 | tf_op jit(solution)/shard_map/ppermute | solution.py:45
  169.3 13.9 %all-to-all-start.2 = ((bf16[4,64,512]{2,1,0:T(8,128)(2,1)}), bf16[4,64,512]{2,1,0:T(8,128)(2,1)S(1)}, u32[]{:S(2)}, u32[]{:S(2)}) async-start(bf16[4,64,512]{2,1,0:T(8,128)(2,1)} %broadcast_in_dim.18), calls=%async_computation.2 | async-start | bytes 524288 | tf_op jit(solution)/shard_map/all_to_all | solution.py:54
  174.7 8.5 %collective-permute-start.18 = (bf16[144,512]{1,0:T(8,128)(2,1)S(1)}, bf16[144,512]{1,0:T(8,128)(2,1)S(1)}, u32[]{:S(2)}, u32[]{:S(2)}) collective-permute-start(bf16[144,512]{1,0:T(8,128)(2,1)S(1)} %get-tuple-element.48), channel_id=1, source_target_pairs={{0,1},{1,2},{2,3},{3,0},{4,5},{5,6},{6,7},{7,4},{8,9},{9,10},{10,1... | collective-permute-start | bytes 442376 | tf_op jit(solution)/shard_map/ppermute | solution.py:45
  (30 other events, 255.9 us)
where the time goes:
time: 193 us; the launch traced here: 192 us
  starting transfers between devices  63.8 us (33%)
  Pallas kernels  59.9 us (31%)
  waiting for transfers between devices  51.9 us (27%)
  local copies, waits for them, and re-layouts  11.7 us (6%)
  other arithmetic  3.62 us (2%)
    ppermute x28, starting transfers between devices, send(): return lax.ppermute(value, ('dp', 'seq'), moves(**shift))  51.1 us
    ppermute x28, waiting for transfers between devices, send(): return lax.ppermute(value, ('dp', 'seq'), moves(**shift))  48.3 us
    pallas_call x1, Pallas kernels, attention(): pl.pallas_call(attn_kernel, grid_spec=pltpu.PrefetchScalarGridSpec(num_sc...  42.3 us
    all_to_all x3, starting transfers between devices, trade(): lax.all_to_all(value, 'dp' if axis == 'y' else 'seq', 0, 0, axis_index_gr...  12.7 us
    pallas_call x2, Pallas kernels, pack(): pl.pallas_call(functools.partial(pack_kernel, groups), grid_spec=pltpu.Pr...  10.4 us
    unnamed x52, local copies, waits for them, and re-layouts  8.76 us
  transfers between devices with their start and end apart: 31, of which 16 were waited for; matrix products, arithmetic and copies ran while one was open for 5% of the time, Pallas kernels for 5%

commit v1 on v0

--- a/solution.py
+++ b/solution.py
@@ -300,18 +300,23 @@
 
 
 def unpack_kernel(sc, s0, s1, s2, s3, out):
-    for kk, group in enumerate(GROUPS[0] + GROUPS[1]):
-        for s, ref in enumerate((s0, s1, s2, s3)):
-            lanes = pl.multiple_of((((sc[3] - s) & 3) * NZ + ((sc[0] + group) & 3)) * PAIR, 128)
-            out[:, pl.ds(lanes, PAIR)] = ref[kk * TOK : kk * TOK + TOK, :]
+    i = pl.program_id(0)
+    for s, ref in enumerate((s0, s1, s2, s3)):
+
+        @pl.when(((sc[3] - s) & 3) == i)
+        def _():
+            for kk, group in enumerate(GROUPS[0] + GROUPS[1]):
+                lanes = pl.multiple_of(((sc[0] + group) & 3) * PAIR, 128)
+                out[:, pl.ds(lanes, PAIR)] = ref[kk * TOK : kk * TOK + TOK, :]
 
 
 def unpack(sc, pieces):
     spec = pl.BlockSpec(memory_space=pltpu.VMEM)
     return pl.pallas_call(
         unpack_kernel,
+        grid=(4,),
         in_specs=[pl.BlockSpec(memory_space=pltpu.SMEM)] + [spec] * 4,
-        out_specs=spec,
+        out_specs=pl.BlockSpec((TOK, NZ * PAIR), lambda i: (0, i)),
         out_shape=jax.ShapeDtypeStruct((TOK, 16 * PAIR), BF),
         cost_estimate=pl.CostEstimate(flops=0, bytes_accessed=3_000_000, transcendentals=0),
         name="unpack",

time: 193 us -> 193 us (level)
  no operation moved by 1% of the time
where the time goes in v1:
time: 193 us; the launch traced here: 192 us
  starting transfers between devices  63.9 us (33%)
  Pallas kernels  60.4 us (31%)
  waiting for transfers between devices  51.3 us (27%)
  local copies, waits for them, and re-layouts  11.7 us (6%)
  other arithmetic  3.62 us (2%)
    ppermute x28, starting transfers between devices, send(): return lax.ppermute(value, ('dp', 'seq'), moves(**shift))  51.2 us
    ppermute x28, waiting for transfers between devices, send(): return lax.ppermute(value, ('dp', 'seq'), moves(**shift))  47.7 us
    pallas_call x1, Pallas kernels, attention(): pl.pallas_call(attn_kernel, grid_spec=pltpu.PrefetchScalarGridSpec(num_sc...  42.3 us
    all_to_all x3, starting transfers between devices, trade(): lax.all_to_all(value, 'dp' if axis == 'y' else 'seq', 0, 0, axis_index_gr...  12.7 us
    pallas_call x2, Pallas kernels, pack(): pl.pallas_call(functools.partial(pack_kernel, groups), grid_spec=pltpu.Pr...  10.4 us
    unnamed x52, local copies, waits for them, and re-layouts  8.76 us
  transfers between devices with their start and end apart: 31, of which 16 were waited for; matrix products, arithmetic and copies ran while one was open for 5% of the time, Pallas kernels for 5%

profile of v1, /device:TPU:40, one launch (start us, length us, event | category | flops | bytes accessed | tf_op | source)
XLA Modules:
  0.0 192.5 jit_solution(17117273752554181644)
XLA Ops:
  1.9 5.2 %pack.2 = bf16[4,272,640]{2,1,0:T(8,128)(2,1)} custom-call(s32[5]{0:T(128)} %stack.19.sc, bf16[128,6144]{1,0:T(8,128)(2,1)} %bitcast.49, bf16[128,6144]{1,0:T(8,128)(2,1)} %bitcast.50, bf16[128,4096]{1,0:T(8,128)(2,1)} %bitcast.53, bf16[128,4096]{1,0:T(8,128)(2,1)} %bitcast.54, bf16[128,4096]{1,0:T(8,128)(2,1)} %bitcast.57, bf16[128,4096]{1,0:T(8,128)(2,1)} %bitcast.58, ...), custom_call_target="tpu_custom_call" | custom-call | flops 2000000 | bytes 4000000 | tf_op jit(solution)/shard_map/pack/pallas_call | solution.py:93
  7.1 4.4 %all-to-all-start = ((bf16[4,272,640]{2,1,0:T(8,128)(2,1)}), bf16[4,272,640]{2,1,0:T(8,128)(2,1)S(1)}, u32[]{:S(2)}, u32[]{:S(2)}) async-start(bf16[4,272,640]{2,1,0:T(8,128)(2,1)} %pack.2), calls=%async_computation | async-start | bytes 2785280 | tf_op jit(solution)/shard_map/all_to_all | solution.py:54
  12.5 3.3 %collective-permute-start.1 = (bf16[144,512]{1,0:T(8,128)(2,1)}, bf16[144,512]{1,0:T(8,128)(2,1)}, u32[]{:S(2)}, u32[]{:S(2)}) collective-permute-start(bf16[144,512]{1,0:T(8,128)(2,1)} %pad_maximum_fusion.1), channel_id=1, source_target_pairs={{0,2},{1,3},{2,0},{3,1},{4,6},{5,7},{6,4},{7,5},{8,10},{9,11},{10,... | collective-permute-start | bytes 442376 | tf_op jit(solution)/shard_map/ppermute | solution.py:45
  15.8 2.8 %collective-permute-start = (bf16[144,512]{1,0:T(8,128)(2,1)}, bf16[144,512]{1,0:T(8,128)(2,1)}, u32[]{:S(2)}, u32[]{:S(2)}) collective-permute-start(bf16[144,512]{1,0:T(8,128)(2,1)} %pad_maximum_fusion.1), channel_id=1, source_target_pairs={{0,1},{1,2},{2,3},{3,0},{4,5},{5,6},{6,7},{7,4},{8,9},{9,10},{10,1... | collective-permute-start | bytes 442376 | tf_op jit(solution)/shard_map/ppermute | solution.py:45
  21.5 5.2 %pack.3 = bf16[4,272,640]{2,1,0:T(8,128)(2,1)} custom-call(s32[5]{0:T(128)} %stack.19.sc, bf16[128,6144]{1,0:T(8,128)(2,1)} %bitcast.51, bf16[128,6144]{1,0:T(8,128)(2,1)} %bitcast.52, bf16[128,4096]{1,0:T(8,128)(2,1)} %bitcast.55, bf16[128,4096]{1,0:T(8,128)(2,1)} %bitcast.56, bf16[128,4096]{1,0:T(8,128)(2,1)} %bitcast.59, bf16[128,4096]{1,0:T(8,128)(2,1)} %bitcast.60, ...), custom_call_target="tpu_custom_call" | custom-call | flops 2000000 | bytes 4000000 | tf_op jit(solution)/shard_map/pack/pallas_call | solution.py:93
  26.7 3.6 %all-to-all-done.refs_0_ = bf16[4,272,640]{2,1,0:T(8,128)(2,1)S(1)} async-done(((bf16[4,272,640]{2,1,0:T(8,128)(2,1)}), bf16[4,272,640]{2,1,0:T(8,128)(2,1)S(1)}, u32[]{:S(2)}, u32[]{:S(2)}) %all-to-all-start) | async-done | bytes 1392672 | tf_op jit(solution)/shard_map/all_to_all | solution.py:54
  30.3 3.5 %all-to-all-start.1 = ((bf16[4,272,640]{2,1,0:T(8,128)(2,1)}), bf16[4,272,640]{2,1,0:T(8,128)(2,1)S(1)}, u32[]{:S(2)}, u32[]{:S(2)}) async-start(bf16[4,272,640]{2,1,0:T(8,128)(2,1)} %pack.3), calls=%async_computation.1 | async-start | bytes 2785280 | tf_op jit(solution)/shard_map/all_to_all | solution.py:54
  39.5 3.0 %collective-permute-start.7 = (bf16[576,512]{1,0:T(8,128)(2,1)}, bf16[576,512]{1,0:T(8,128)(2,1)S(1)}, u32[]{:S(2)}, u32[]{:S(2)}) collective-permute-start(bf16[576,512]{1,0:T(8,128)(2,1)} %constant_dynamic-update-slice_fusion.refs_2_), channel_id=1, source_target_pairs={{0,12},{1,13},{2,14},{3,15},{4,0},{5,1},{6,2},{7,3},{8,4},{9,5},{1... | collective-permute-start | bytes 1769480 | tf_op jit(solution)/shard_map/ppermute | solution.py:45
  44.2 4.6 %collective-permute-start.8 = (bf16[256,512]{1,0:T(8,128)(2,1)S(1)}, bf16[256,512]{1,0:T(8,128)(2,1)S(1)}, u32[]{:S(2)}, u32[]{:S(2)}) collective-permute-start(bf16[256,512]{1,0:T(8,128)(2,1)S(1)} %get-tuple-element.52), channel_id=1, source_target_pairs={{0,34},{1,35},{2,0},{3,1},{4,38},{5,39},{6,4},{7,5},{8,42},{9,43},... | collective-permute-start | bytes 786440 | tf_op jit(solution)/shard_map/ppermute | solution.py:45
  48.7 9.2 %collective-permute-done.8 = bf16[256,512]{1,0:T(8,128)(2,1)S(1)} collective-permute-done((bf16[256,512]{1,0:T(8,128)(2,1)S(1)}, bf16[256,512]{1,0:T(8,128)(2,1)S(1)}, u32[]{:S(2)}, u32[]{:S(2)}) %collective-permute-start.8) | collective-permute-done | bytes 262176 | tf_op jit(solution)/shard_map/ppermute | solution.py:45
  58.8 6.4 %collective-permute-done.7.refs_5_ = bf16[576,512]{1,0:T(8,128)(2,1)S(1)} collective-permute-done((bf16[576,512]{1,0:T(8,128)(2,1)}, bf16[576,512]{1,0:T(8,128)(2,1)S(1)}, u32[]{:S(2)}, u32[]{:S(2)}) %collective-permute-start.7) | collective-permute-done | bytes 589856 | tf_op jit(solution)/shard_map/ppermute | solution.py:45
  67.6 9.2 %collective-permute-done.5.refs_3_ = bf16[576,512]{1,0:T(8,128)(2,1)} collective-permute-done((bf16[576,512]{1,0:T(8,128)(2,1)}, bf16[576,512]{1,0:T(8,128)(2,1)}, u32[]{:S(2)}, u32[]{:S(2)}) %collective-permute-start.5) | collective-permute-done | bytes 589856 | tf_op jit(solution)/shard_map/ppermute | solution.py:45
  77.9 42.3 %attention.1 = (bf16[512,384]{1,0:T(8,128)(2,1)}, bf16[512,384]{1,0:T(8,128)(2,1)}, bf16[512,384]{1,0:T(8,128)(2,1)}, bf16[512,384]{1,0:T(8,128)(2,1)}, bf16[576...) custom-call(s32[5]{0:T(128)} %stack.19.sc, ...), custom_call_target="tpu_custom_call" | custom-call | flops 49999998976 | bytes 14000000 | tf_op jit(solution)/shard_map/attention/pallas_call | solution.py:289
  120.3 2.9 %collective-permute-done.19 = bf16[4,4,64,512]{3,2,1,0:T(8,128)(2,1)S(1)} collective-permute-done((bf16[4,4,64,512]{3,2,1,0:T(8,128)(2,1)}, bf16[4,4,64,512]{3,2,1,0:T(8,128)(2,1)S(1)}, u32[]{:S(2)}, u32[]{:S(2)}) %collective-permute-start.19) | collective-permute-done | bytes 1048608 | tf_op jit(solution)/shard_map/ppermute | solution.py:45
  127.0 2.3 %collective-permute-start.21 = (bf16[4,64,512]{2,1,0:T(8,128)(2,1)S(1)}, bf16[4,64,512]{2,1,0:T(8,128)(2,1)S(1)}, u32[]{:S(2)}, u32[]{:S(2)}) collective-permute-start(bf16[4,64,512]{2,1,0:T(8,128)(2,1)S(1)} %get-tuple-element.47), channel_id=1, source_target_pairs={{0,128},{1,129},{2,130},{3,131},{4,132},{5,133},{6,134},{7,135},{8... | collective-permute-start | bytes 786440 | tf_op jit(solution)/shard_map/ppermute | solution.py:45
  134.2 2.2 %collective-permute-start.15 = (bf16[576,512]{1,0:T(8,128)(2,1)S(1)}, bf16[576,512]{1,0:T(8,128)(2,1)S(1)}, u32[]{:S(2)}, u32[]{:S(2)}) collective-permute-start(bf16[576,512]{1,0:T(8,128)(2,1)S(1)} %copy-done.13), channel_id=1, source_target_pairs={{0,12},{1,13},{2,14},{3,15},{4,0},{5,1},{6,2},{7,3},{8,4},{9,5},{1... | collective-permute-start | bytes 1769480 | tf_op jit(solution)/shard_map/ppermute | solution.py:45
  136.4 4.6 %collective-permute-done.21 = bf16[4,64,512]{2,1,0:T(8,128)(2,1)S(1)} collective-permute-done((bf16[4,64,512]{2,1,0:T(8,128)(2,1)S(1)}, bf16[4,64,512]{2,1,0:T(8,128)(2,1)S(1)}, u32[]{:S(2)}, u32[]{:S(2)}) %collective-permute-start.21) | collective-permute-done | bytes 262176 | tf_op jit(solution)/shard_map/ppermute | solution.py:45
  145.5 4.0 %collective-permute-start.24 = (bf16[64,512]{1,0:T(8,128)(2,1)S(1)}, bf16[64,512]{1,0:T(8,128)(2,1)S(1)}, u32[]{:S(2)}, u32[]{:S(2)}) collective-permute-start(bf16[64,512]{1,0:T(8,128)(2,1)S(1)} %get-tuple-element.56), channel_id=1, source_target_pairs={{0,2},{1,3},{2,32},{3,33},{4,6},{5,7},{6,36},{7,37},{8,10},{9,11},... | collective-permute-start | bytes 196616 | tf_op jit(solution)/shard_map/ppermute | solution.py:45
  151.2 2.6 %collective-permute-done.24 = bf16[64,512]{1,0:T(8,128)(2,1)S(1)} collective-permute-done((bf16[64,512]{1,0:T(8,128)(2,1)S(1)}, bf16[64,512]{1,0:T(8,128)(2,1)S(1)}, u32[]{:S(2)}, u32[]{:S(2)}) %collective-permute-start.24) | collective-permute-done | bytes 65568 | tf_op jit(solution)/shard_map/ppermute | solution.py:45
  154.4 3.5 %collective-permute-start.12 = (bf16[512,384]{1,0:T(8,128)(2,1)S(1)}, bf16[512,384]{1,0:T(8,128)(2,1)S(1)}, u32[]{:S(2)}, u32[]{:S(2)}) collective-permute-start(bf16[512,384]{1,0:T(8,128)(2,1)S(1)} %copy-done.18), channel_id=1, source_target_pairs={{0,12},{1,13},{2,14},{3,15},{4,0},{5,1},{6,2},{7,3},{8,4},{9,5},{1... | collective-permute-start | bytes 1179656 | tf_op jit(solution)/shard_map/ppermute | solution.py:45
  160.0 6.3 %collective-permute-start.26 = (bf16[64,512]{1,0:T(8,128)(2,1)S(1)}, bf16[64,512]{1,0:T(8,128)(2,1)S(1)}, u32[]{:S(2)}, u32[]{:S(2)}) collective-permute-start(bf16[64,512]{1,0:T(8,128)(2,1)S(1)} %fusion.5), channel_id=1, source_target_pairs={{0,32},{1,33},{2,34},{3,35},{4,36},{5,37},{6,38},{7,39},{8,40},{9,... | collective-permute-start | bytes 196616 | tf_op jit(solution)/shard_map/ppermute | solution.py:45
  169.3 4.7 %all-to-all-start.2 = ((bf16[4,64,512]{2,1,0:T(8,128)(2,1)}), bf16[4,64,512]{2,1,0:T(8,128)(2,1)S(1)}, u32[]{:S(2)}, u32[]{:S(2)}) async-start(bf16[4,64,512]{2,1,0:T(8,128)(2,1)} %broadcast_in_dim.18), calls=%async_computation.2 | async-start | bytes 524288 | tf_op jit(solution)/shard_map/all_to_all | solution.py:54
  180.5 3.1 %unpack.1 = bf16[128,6144]{1,0:T(8,128)(2,1)} custom-call(s32[5]{0:T(128)} %stack.19.sc, bf16[512,384]{1,0:T(8,128)(2,1)} %get-tuple-element.31.s0, bf16[512,384]{1,0:T(8,128)(2,1)} %copy-done.6, bf16[512,384]{1,0:T(8,128)(2,1)} %copy-done.7, bf16[512,384]{1,0:T(8,128)(2,1)} %copy-done.8), custom_call_target="tpu_custom_call" | custom-call | bytes 3000000 | tf_op jit(solution)/shard_map/unpack/pallas_call | solution.py:315
  190.0 2.5 %place_weights.1 = (f32[512,2,128]{2,1,0:T(2,128)}, f32[512,2,128]{2,1,0:T(2,128)}) custom-call(s32[5]{0:T(128)} %stack.19.sc, bf16[256,512]{1,0:T(8,128)(2,1)} %bitcast.63, bf16[256,512]{1,0:T(8,128)(2,1)} %copy-done.9), custom_call_target="tpu_custom_call" | custom-call | bytes 2000000 | tf_op jit(solution)/shard_map/place_weights/pallas_call | solution.py:355
  (113 shorter events, 49.4 us)
Async XLA Ops:
  7.1 23.2 %all-to-all-start = ((bf16[4,272,640]{2,1,0:T(8,128)(2,1)}), bf16[4,272,640]{2,1,0:T(8,128)(2,1)S(1)}, u32[]{:S(2)}, u32[]{:S(2)}) async-start(bf16[4,272,640]{2,1,0:T(8,128)(2,1)} %pack.2), calls=%async_computation | async-start | bytes 2785280 | tf_op jit(solution)/shard_map/all_to_all | solution.py:54
  12.4 25.2 %collective-permute-start.2 = (bf16[144,512]{1,0:T(8,128)(2,1)}, bf16[144,512]{1,0:T(8,128)(2,1)S(1)}, u32[]{:S(2)}, u32[]{:S(2)}) collective-permute-start(bf16[144,512]{1,0:T(8,128)(2,1)} %pad_maximum_fusion.1), channel_id=1, source_target_pairs={{0,3},{1,0},{2,1},{3,2},{4,7},{5,4},{6,5},{7,6},{8,11},{9,8},{10,9... | collective-permute-start | bytes 442376 | tf_op jit(solution)/shard_map/ppermute | solution.py:45
  12.5 23.5 %collective-permute-start.1 = (bf16[144,512]{1,0:T(8,128)(2,1)}, bf16[144,512]{1,0:T(8,128)(2,1)}, u32[]{:S(2)}, u32[]{:S(2)}) collective-permute-start(bf16[144,512]{1,0:T(8,128)(2,1)} %pad_maximum_fusion.1), channel_id=1, source_target_pairs={{0,2},{1,3},{2,0},{3,1},{4,6},{5,7},{6,4},{7,5},{8,10},{9,11},{10,... | collective-permute-start | bytes 442376 | tf_op jit(solution)/shard_map/ppermute | solution.py:45
  15.8 18.6 %collective-permute-start = (bf16[144,512]{1,0:T(8,128)(2,1)}, bf16[144,512]{1,0:T(8,128)(2,1)}, u32[]{:S(2)}, u32[]{:S(2)}) collective-permute-start(bf16[144,512]{1,0:T(8,128)(2,1)} %pad_maximum_fusion.1), channel_id=1, source_target_pairs={{0,1},{1,2},{2,3},{3,0},{4,5},{5,6},{6,7},{7,4},{8,9},{9,10},{10,1... | collective-permute-start | bytes 442376 | tf_op jit(solution)/shard_map/ppermute | solution.py:45
  18.7 20.7 %collective-permute-start.4 = (bf16[512,512]{1,0:T(8,128)(2,1)S(1)}, bf16[512,512]{1,0:T(8,128)(2,1)}, u32[]{:S(2)}, u32[]{:S(2)}) collective-permute-start(bf16[512,512]{1,0:T(8,128)(2,1)S(1)} %bitcast_dynamic-update-slice_fusion.refs_6_), channel_id=1, source_target_pairs={{0,1},{1,2},{2,3},{3,32},{4,5},{5,6},{6,7},{7,36},{8,9},{9,10},{10... | collective-permute-start | bytes 1572872 | tf_op jit(solution)/shard_map/ppermute | solution.py:45
  18.8 20.6 %collective-permute-start.3 = (bf16[512,512]{1,0:T(8,128)(2,1)S(1)}, bf16[512,512]{1,0:T(8,128)(2,1)}, u32[]{:S(2)}, u32[]{:S(2)}) collective-permute-start(bf16[512,512]{1,0:T(8,128)(2,1)S(1)} %bitcast_dynamic-update-slice_fusion.refs_6_), channel_id=1, source_target_pairs={{0,35},{1,0},{2,1},{3,2},{4,39},{5,4},{6,5},{7,6},{8,43},{9,8},{10... | collective-permute-start | bytes 1572872 | tf_op jit(solution)/shard_map/ppermute | solution.py:45
  30.3 46.5 %all-to-all-start.1 = ((bf16[4,272,640]{2,1,0:T(8,128)(2,1)}), bf16[4,272,640]{2,1,0:T(8,128)(2,1)S(1)}, u32[]{:S(2)}, u32[]{:S(2)}) async-start(bf16[4,272,640]{2,1,0:T(8,128)(2,1)} %pack.3), calls=%async_computation.1 | async-start | bytes 2785280 | tf_op jit(solution)/shard_map/all_to_all | solution.py:54
  39.5 25.8 %collective-permute-start.7 = (bf16[576,512]{1,0:T(8,128)(2,1)}, bf16[576,512]{1,0:T(8,128)(2,1)S(1)}, u32[]{:S(2)}, u32[]{:S(2)}) collective-permute-start(bf16[576,512]{1,0:T(8,128)(2,1)} %constant_dynamic-update-slice_fusion.refs_2_), channel_id=1, source_target_pairs={{0,12},{1,13},{2,14},{3,15},{4,0},{5,1},{6,2},{7,3},{8,4},{9,5},{1... | collective-permute-start | bytes 1769480 | tf_op jit(solution)/shard_map/ppermute | solution.py:45
  42.4 24.3 %collective-permute-start.6 = (bf16[576,512]{1,0:T(8,128)(2,1)}, bf16[576,512]{1,0:T(8,128)(2,1)S(1)}, u32[]{:S(2)}, u32[]{:S(2)}) collective-permute-start(bf16[576,512]{1,0:T(8,128)(2,1)} %constant_dynamic-update-slice_fusion.refs_2_), channel_id=1, source_target_pairs={{0,8},{1,9},{2,10},{3,11},{4,12},{5,13},{6,14},{7,15},{8,0},{9,1},... | collective-permute-start | bytes 1769480 | tf_op jit(solution)/shard_map/ppermute | solution.py:45
  43.3 33.5 %collective-permute-start.5 = (bf16[576,512]{1,0:T(8,128)(2,1)}, bf16[576,512]{1,0:T(8,128)(2,1)}, u32[]{:S(2)}, u32[]{:S(2)}) collective-permute-start(bf16[576,512]{1,0:T(8,128)(2,1)} %constant_dynamic-update-slice_fusion.refs_2_), channel_id=1, source_target_pairs={{0,4},{1,5},{2,6},{3,7},{4,8},{5,9},{6,10},{7,11},{8,12},{9,13},{1... | collective-permute-start | bytes 1769480 | tf_op jit(solution)/shard_map/ppermute | solution.py:45
  44.2 13.7 %collective-permute-start.8 = (bf16[256,512]{1,0:T(8,128)(2,1)S(1)}, bf16[256,512]{1,0:T(8,128)(2,1)S(1)}, u32[]{:S(2)}, u32[]{:S(2)}) collective-permute-start(bf16[256,512]{1,0:T(8,128)(2,1)S(1)} %get-tuple-element.52), channel_id=1, source_target_pairs={{0,34},{1,35},{2,0},{3,1},{4,38},{5,39},{6,4},{7,5},{8,42},{9,43},... | collective-permute-start | bytes 786440 | tf_op jit(solution)/shard_map/ppermute | solution.py:45
  48.7 9.3 %collective-permute-start.9 = (bf16[256,512]{1,0:T(8,128)(2,1)S(1)}, bf16[256,512]{1,0:T(8,128)(2,1)S(1)}, u32[]{:S(2)}, u32[]{:S(2)}) collective-permute-start(bf16[256,512]{1,0:T(8,128)(2,1)S(1)} %get-tuple-element.53), channel_id=1, source_target_pairs={{0,2},{1,3},{2,32},{3,33},{4,6},{5,7},{6,36},{7,37},{8,10},{9,11},... | collective-permute-start | bytes 786440 | tf_op jit(solution)/shard_map/ppermute | solution.py:45
  124.9 9.2 %collective-permute-start.20 = (bf16[4,64,512]{2,1,0:T(8,128)(2,1)S(1)}, bf16[4,64,512]{2,1,0:T(8,128)(2,1)S(1)}, u32[]{:S(2)}, u32[]{:S(2)}) collective-permute-start(bf16[4,64,512]{2,1,0:T(8,128)(2,1)S(1)} %get-tuple-element.45), channel_id=1, source_target_pairs={{0,64},{1,65},{2,66},{3,67},{4,68},{5,69},{6,70},{7,71},{8,72},{9,... | collective-permute-start | bytes 786440 | tf_op jit(solution)/shard_map/ppermute | solution.py:45
  126.6 9.8 %collective-permute-start.22 = (bf16[4,64,512]{2,1,0:T(8,128)(2,1)S(1)}, bf16[4,64,512]{2,1,0:T(8,128)(2,1)S(1)}, u32[]{:S(2)}, u32[]{:S(2)}) collective-permute-start(bf16[4,64,512]{2,1,0:T(8,128)(2,1)S(1)} %get-tuple-element.46), channel_id=1, source_target_pairs={{0,192},{1,193},{2,194},{3,195},{4,196},{5,197},{6,198},{7,199},{8... | collective-permute-start | bytes 786440 | tf_op jit(solution)/shard_map/ppermute | solution.py:45
  127.0 14.0 %collective-permute-start.21 = (bf16[4,64,512]{2,1,0:T(8,128)(2,1)S(1)}, bf16[4,64,512]{2,1,0:T(8,128)(2,1)S(1)}, u32[]{:S(2)}, u32[]{:S(2)}) collective-permute-start(bf16[4,64,512]{2,1,0:T(8,128)(2,1)S(1)} %get-tuple-element.47), channel_id=1, source_target_pairs={{0,128},{1,129},{2,130},{3,131},{4,132},{5,133},{6,134},{7,135},{8... | collective-permute-start | bytes 786440 | tf_op jit(solution)/shard_map/ppermute | solution.py:45
  129.3 25.0 %collective-permute-start.13 = (bf16[576,512]{1,0:T(8,128)(2,1)S(1)}, bf16[576,512]{1,0:T(8,128)(2,1)S(1)}, u32[]{:S(2)}, u32[]{:S(2)}) collective-permute-start(bf16[576,512]{1,0:T(8,128)(2,1)S(1)} %copy-done.15), channel_id=1, source_target_pairs={{0,4},{1,5},{2,6},{3,7},{4,8},{5,9},{6,10},{7,11},{8,12},{9,13},{1... | collective-permute-start | bytes 1769480 | tf_op jit(solution)/shard_map/ppermute | solution.py:45
  131.0 29.0 %collective-permute-start.14 = (bf16[576,512]{1,0:T(8,128)(2,1)S(1)}, bf16[576,512]{1,0:T(8,128)(2,1)S(1)}, u32[]{:S(2)}, u32[]{:S(2)}) collective-permute-start(bf16[576,512]{1,0:T(8,128)(2,1)S(1)} %copy-done.14), channel_id=1, source_target_pairs={{0,8},{1,9},{2,10},{3,11},{4,12},{5,13},{6,14},{7,15},{8,0},{9,1},... | collective-permute-start | bytes 1769480 | tf_op jit(solution)/shard_map/ppermute | solution.py:45
  134.2 32.1 %collective-permute-start.15 = (bf16[576,512]{1,0:T(8,128)(2,1)S(1)}, bf16[576,512]{1,0:T(8,128)(2,1)S(1)}, u32[]{:S(2)}, u32[]{:S(2)}) collective-permute-start(bf16[576,512]{1,0:T(8,128)(2,1)S(1)} %copy-done.13), channel_id=1, source_target_pairs={{0,12},{1,13},{2,14},{3,15},{4,0},{5,1},{6,2},{7,3},{8,4},{9,5},{1... | collective-permute-start | bytes 1769480 | tf_op jit(solution)/shard_map/ppermute | solution.py:45
  149.5 29.2 %collective-permute-start.10 = (bf16[512,384]{1,0:T(8,128)(2,1)}, bf16[512,384]{1,0:T(8,128)(2,1)S(1)}, u32[]{:S(2)}, u32[]{:S(2)}) collective-permute-start(bf16[512,384]{1,0:T(8,128)(2,1)} %get-tuple-element.32), channel_id=1, source_target_pairs={{0,4},{1,5},{2,6},{3,7},{4,8},{5,9},{6,10},{7,11},{8,12},{9,13},{1... | collective-permute-start | bytes 1179656 | tf_op jit(solution)/shard_map/ppermute | solution.py:45
  153.8 25.8 %collective-permute-start.11 = (bf16[512,384]{1,0:T(8,128)(2,1)S(1)}, bf16[512,384]{1,0:T(8,128)(2,1)S(1)}, u32[]{:S(2)}, u32[]{:S(2)}) collective-permute-start(bf16[512,384]{1,0:T(8,128)(2,1)S(1)} %copy-done.19), channel_id=1, source_target_pairs={{0,8},{1,9},{2,10},{3,11},{4,12},{5,13},{6,14},{7,15},{8,0},{9,1},... | collective-permute-start | bytes 1179656 | tf_op jit(solution)/shard_map/ppermute | solution.py:45
  154.4 25.2 %collective-permute-start.12 = (bf16[512,384]{1,0:T(8,128)(2,1)S(1)}, bf16[512,384]{1,0:T(8,128)(2,1)S(1)}, u32[]{:S(2)}, u32[]{:S(2)}) collective-permute-start(bf16[512,384]{1,0:T(8,128)(2,1)S(1)} %copy-done.18), channel_id=1, source_target_pairs={{0,12},{1,13},{2,14},{3,15},{4,0},{5,1},{6,2},{7,3},{8,4},{9,5},{1... | collective-permute-start | bytes 1179656 | tf_op jit(solution)/shard_map/ppermute | solution.py:45
  160.0 8.5 %collective-permute-start.26 = (bf16[64,512]{1,0:T(8,128)(2,1)S(1)}, bf16[64,512]{1,0:T(8,128)(2,1)S(1)}, u32[]{:S(2)}, u32[]{:S(2)}) collective-permute-start(bf16[64,512]{1,0:T(8,128)(2,1)S(1)} %fusion.5), channel_id=1, source_target_pairs={{0,32},{1,33},{2,34},{3,35},{4,36},{5,37},{6,38},{7,39},{8,40},{9,... | collective-permute-start | bytes 196616 | tf_op jit(solution)/shard_map/ppermute | solution.py:45
  169.3 14.4 %all-to-all-start.2 = ((bf16[4,64,512]{2,1,0:T(8,128)(2,1)}), bf16[4,64,512]{2,1,0:T(8,128)(2,1)S(1)}, u32[]{:S(2)}, u32[]{:S(2)}) async-start(bf16[4,64,512]{2,1,0:T(8,128)(2,1)} %broadcast_in_dim.18), calls=%async_computation.2 | async-start | bytes 524288 | tf_op jit(solution)/shard_map/all_to_all | solution.py:54
  174.7 9.1 %collective-permute-start.18 = (bf16[144,512]{1,0:T(8,128)(2,1)S(1)}, bf16[144,512]{1,0:T(8,128)(2,1)S(1)}, u32[]{:S(2)}, u32[]{:S(2)}) collective-permute-start(bf16[144,512]{1,0:T(8,128)(2,1)S(1)} %get-tuple-element.48), channel_id=1, source_target_pairs={{0,1},{1,2},{2,3},{3,0},{4,5},{5,6},{6,7},{7,4},{8,9},{9,10},{10,1... | collective-permute-start | bytes 442376 | tf_op jit(solution)/shard_map/ppermute | solution.py:45
  (30 other events, 254.4 us)
